TPU v7x, 32 devices: a whole 2x2x4 slice. The times are simulated.
32 devices in a mesh: parts: 2 (over x), row: 16 (over z, y, core).
Axes of the slice: x: 2, y: 2, z: 4, core: 2. Of those that a mesh axis runs over, the one named last changes fastest.
Arguments:
- audio: bfloat16 [8388608], P(('parts', 'row')), parts along dimension 0, may hold values from -8 to 8
- templates: bfloat16 [8192, 512], P(('parts', 'row')), parts along dimension 0, may hold values from 0.025 to 4, as said below
- activations: bfloat16 [4096, 512], P(('parts', 'row')), parts along dimension 0, may hold values from 0.025 to 4, as said below
Outputs:
- h_new: bfloat16 [4096, 512], P(('parts', 'row')), parts along dimension 0
- w_new: bfloat16 [8192, 512], P(('parts', 'row')), parts along dimension 0
There are 2 independent parts, one for each index of `parts`. A program takes and returns all parts, laid end to end along the dimension named above; each array names one. Nothing has to cross between parts.
Inputs may be any that keep to these rules, and one draw needn't show every extreme that they name: `templates`: positive entries. `activations`: positive entries.
All inputs are finite; a program needn't handle non-finite values.
Results may differ from a plain program's by a relative error of at most 0.0034.
Values may be sent and summed in bfloat16 or wider, within the bound.
A program may use at most 64 MiB of HBM per device.

v0:
```python
import math

import jax
import jax.numpy as jnp
from jax import lax
from jax.sharding import PartitionSpec as P

NFFT = 8192
BINS = 4096
HOP = 2048


radix = 128


def shifted(value, axis, by):
    length = lax.axis_size(axis)
    pairs = [(i, i + by) for i in range(length) if 0 <= i + by < length]
    return lax.ppermute(value, axis, pairs)


def dft_tables(length):
    inner_len = length // radix
    half_len = inner_len // 2
    outer_idx = jnp.arange(radix, dtype=jnp.int32)
    inner_idx = jnp.arange(inner_len, dtype=jnp.int32)
    upper_idx = jnp.arange(half_len, dtype=jnp.int32)
    angle_one = (outer_idx[:, None] * outer_idx[None, :] % radix).astype(jnp.float32) * (
        2.0 * math.pi / radix
    )
    section_one = jnp.concatenate([jnp.cos(angle_one), -jnp.sin(angle_one)], axis=1).astype(
        jnp.bfloat16
    )
    angle_twid = (inner_idx[:, None] * outer_idx[None, :] % length).astype(jnp.float32) * (
        2.0 * math.pi / length
    )
    angle_two = (inner_idx[:, None] * upper_idx[None, :] % inner_len).astype(jnp.float32) * (
        2.0 * math.pi / inner_len
    )
    cos_two = jnp.cos(angle_two)
    sin_two = jnp.sin(angle_two)
    upper_half = jnp.concatenate([cos_two, -sin_two], axis=1)
    lower_half = jnp.concatenate([sin_two, cos_two], axis=1)
    section_two = jnp.concatenate([upper_half, lower_half], axis=0).astype(jnp.bfloat16)
    sample_idx = jnp.arange(length, dtype=jnp.int32).astype(jnp.float32)
    hann_window = 0.5 - 0.5 * jnp.cos(sample_idx * (2.0 * math.pi / length))
    return (hann_window, section_one, jnp.cos(angle_twid), jnp.sin(angle_twid), section_two)


def magnitudes(windowed, tables_all):
    hann_window, section_one, twid_cos, twid_sin, section_two = tables_all
    frame_count = windowed.shape[0]
    length = windowed.shape[1]
    inner_len = section_two.shape[0] // 2
    half_len = inner_len // 2
    shaped = windowed.reshape(frame_count, radix, inner_len)
    section_out = jnp.einsum("nab,ac->nbc", shaped, section_one, preferred_element_type=jnp.float32)
    real_y = section_out[:, :, :radix]
    imag_y = section_out[:, :, radix:]
    real_z = (real_y * twid_cos + imag_y * twid_sin).astype(jnp.bfloat16)
    imag_z = (imag_y * twid_cos - real_y * twid_sin).astype(jnp.bfloat16)
    stacked = jnp.concatenate([real_z, imag_z], axis=1)
    second = jnp.einsum("nbk,bm->nmk", stacked, section_two, preferred_element_type=jnp.float32)
    real_x = second[:, :half_len, :]
    imag_x = second[:, half_len:, :]
    level = jnp.sqrt(real_x * real_x + imag_x * imag_x) * (16.0 / math.sqrt(length))
    return level.reshape(frame_count, half_len * radix).astype(jnp.bfloat16)


def inner_rows(left, right):
    return lax.dot_general(
        left, right, (((0,), (0,)), ((), ())), preferred_element_type=jnp.float32
    )


def refine(factor, numer, gram_low):
    denom = jnp.dot(factor, gram_low, preferred_element_type=jnp.float32)
    return (factor.astype(jnp.float32) * numer / denom).astype(jnp.bfloat16)


def own_gram(factor):
    return lax.psum(inner_rows(factor, factor), "row")


def shards(audio, templates, activations):
    frame_count = activations.shape[0]
    tables_all = dft_tables(NFFT)
    tail_audio = shifted(audio[: 3 * HOP], "row", -1)
    frame_rows = jnp.concatenate([audio, tail_audio]).reshape(frame_count + 3, HOP)
    block_len = math.gcd(frame_count, 16)

    def one_block(block_index):
        window_rows = lax.dynamic_slice_in_dim(
            frame_rows, block_index * block_len, block_len + 3, 0
        )
        frames = jnp.concatenate(
            [window_rows[offset : offset + block_len] for offset in range(4)], axis=1
        )
        windowed = (frames.astype(jnp.float32) * tables_all[0]).astype(jnp.bfloat16)
        return magnitudes(windowed, tables_all)

    blocks_out = lax.map(one_block, jnp.arange(frame_count // block_len, dtype=jnp.int32))
    spectrogram = blocks_out.reshape(frame_count, BINS)
    gram_w = lax.psum(inner_rows(templates, templates), "row").astype(jnp.bfloat16)
    columns = lax.all_to_all(spectrogram, "row", split_axis=1, concat_axis=0, tiled=True)
    num_h = lax.psum_scatter(
        jnp.dot(columns, templates, preferred_element_type=jnp.float32),
        "row",
        scatter_dimension=0,
        tiled=True,
    )
    h_new = refine(activations, num_h, gram_w)
    num_acc = inner_rows(columns, lax.all_gather(h_new, "row", axis=0, tiled=True))
    gram_h = own_gram(h_new)
    w_new = refine(templates, num_acc, gram_h.astype(jnp.bfloat16))
    return (h_new, w_new)


def solution(mesh):
    in_specs = (P(("parts", "row")), P(("parts", "row"), None), P(("parts", "row"), None))
    out_specs = (P(("parts", "row"), None), P(("parts", "row"), None))
    return jax.shard_map(shards, mesh=mesh, in_specs=in_specs, out_specs=out_specs, check_vma=False)
```

profile of v0, /device:TPU:0, one launch (start us, length us, event | category | flops | bytes accessed | tf_op | source)
XLA Modules:
  0.0 247.9 jit_solution(15002197036663116856)
XLA Ops:
  7.2 0.7 slice.27
  7.9 1.3 collective-permute-start
  9.8 1.2 collective-permute-done
  11.0 1.1 pad_maximum_fusion
  12.3 34.5 %while.12 = (s32[]{:T(128)}, bf16[8,16,4096]{2,1,0:T(8,128)(2,1)S(1)}, s32[8]{0:T(128)S(1)}, bf16[131,2048]{1,0:T(8,128)(2,1)S(1)}, bf16[128,256]{1,0:T(8,128)(2...) while((s32[]{:T(128)}, ...), condition=%wide.region_1.2_spmd.clone.clone, body=%wide.region_0.1_spmd.clone.clone.sunk | while | flops 104546312 | bytes 7094511 | solution.py:102
  12.3 0.6 dynamic_slice.12
  15.4 0.5 fusion.78
  16.7 0.6 dynamic_slice.12
  19.7 0.5 fusion.78
  21.0 0.6 dynamic_slice.12
  24.0 0.5 fusion.78
  25.3 0.6 dynamic_slice.12
  28.3 0.5 fusion.78
  29.6 0.6 dynamic_slice.12
  32.7 0.5 fusion.78
  33.9 0.6 dynamic_slice.12
  37.0 0.5 fusion.78
  38.2 0.6 dynamic_slice.12
  41.3 0.5 fusion.78
  42.5 0.6 dynamic_slice.12
  45.6 0.5 fusion.78
  47.1 0.3 copy.31
  47.5 33.3 %all_to_all.19 = bf16[128,16,256]{2,0,1:T(8,128)(2,1)S(1)} all-to-all(bf16[128,16,256]{2,0,1:T(8,128)(2,1)S(1)} %copy.31), channel_id=1, replica_groups=mesh['parts'=2,'row'=16] {'row'}, dimensions={1} | all-to-all | bytes 2097152 | tf_op jit(solution)/shard_map/all_to_all | solution.py:105
  80.8 2.7 %fusion.54 = f32[2048,512]{1,0:T(8,128)} fusion(bf16[2048,256]{1,0:T(8,128)(2,1)S(1)} %bitcast.43, bf16[256,512]{1,0:T(8,128)(2,1)S(1)} %copy-done), kind=kOutput, calls=%fused_computation.82 | convolution fusion | flops 536870912 | bytes 5505024 | tf_op jit(solution)/shard_map/dot_general | solution.py:107
  83.5 0.3 fusion.55
  83.8 78.2 %all-reduce.2 = bf16[512,512]{1,0:T(8,128)(2,1)S(1)} all-reduce(f32[512,512]{1,0:T(8,128)S(1)} %fusion.55), channel_id=1, replica_groups=mesh['parts'=2,'row'=16] {'row'}, use_global_device_ids=true, to_apply=%region_3.4 | all-reduce | flops 262144 | bytes 1572864 | tf_op jit(solution)/shard_map/psum | solution.py:104
  162.0 1.6 reduce-scatter.2.cloned.1.call-done
  163.6 1.8 fusion.37
  165.5 1.3 fusion.56
  166.8 70.9 %all-reduce.3 = bf16[512,512]{1,0:T(8,128)(2,1)S(1)} all-reduce(f32[512,512]{1,0:T(8,128)S(1)} %fusion.56), channel_id=1, replica_groups=mesh['parts'=2,'row'=16] {'row'}, use_global_device_ids=true, to_apply=%region_4.5 | all-reduce | flops 262144 | bytes 1572864 | tf_op jit(solution)/shard_map/psum | solution.py:82
  237.7 0.3 convolution_bitcast_fusion.1
  238.1 3.0 %fusion.35 = bf16[256,512]{1,0:T(8,128)(2,1)} fusion(f32[256,512]{1,0:T(8,128)S(1)} %convolution_bitcast_fusion.1, bf16[2048,256]{1,0:T(8,128)(2,1)S(1)} %bitcast.44, bf16[2048,512]{1,0:T(8,128)(2,1)} %all-gather.2.cloned.1.call-done, bf16[256,512]{1,0:T(8,128)(2,1)S(1)} %copy-done), kind=kOutput, calls=%fused_computation.49 | convolution fusion | flops 537395200 | bytes 4194304 | tf_op jit(solution)/shard_map/dot_general | solution.py:71
  (162 shorter events, 20.7 us)
Async XLA Ops:
  7.2 156.5 %reduce-scatter.2.cloned.1.call-start = ((), (), s32[]{:S(2)}) async-start(), calls=%async_computation.2 | async-start | bytes 4456448 | tf_op jit(solution)/shard_map/reduce_scatter | solution.py:106
  7.9 3.1 %collective-permute-start = (bf16[6144]{0:T(1024)(128)(2,1)S(1)}, bf16[6144]{0:T(1024)(128)(2,1)S(1)}, u32[]{:S(2)}, u32[]{:S(2)}) collective-permute-start(bf16[6144]{0:T(1024)(128)(2,1)S(1)} %slice.27), channel_id=1, source_target_pairs={{1,0},{2,1},{3,2},{4,3},{5,4},{6,5},{7,6},{8,7},{9,8},{10,9},{11,1... | collective-permute-start | bytes 36872 | tf_op jit(solution)/shard_map/ppermute | solution.py:19
  47.1 33.7 %copy-start = (bf16[256,512]{1,0:T(8,128)(2,1)S(1)}, bf16[256,512]{1,0:T(8,128)(2,1)}, u32[]{:S(2)}) copy-start(bf16[256,512]{1,0:T(8,128)(2,1)} %param.6) | copy-start | bytes 786436
  83.4 80.2 %copy-start.1 = (bf16[128,512]{1,0:T(8,128)(2,1)S(1)}, bf16[128,512]{1,0:T(8,128)(2,1)}, u32[]{:S(2)}) copy-start(bf16[128,512]{1,0:T(8,128)(2,1)} %param.7) | copy-start | bytes 393220
  83.4 154.6 %all-gather.2.cloned.1.call-start = ((), (), s32[]{:S(2)}) async-start(), calls=%async_computation.3 | async-start | bytes 2228224 | tf_op jit(solution)/shard_map/all_gather | solution.py:113
Sparse Core Ops, SparseCore 0:
  83.6 80.0 reduce-scatter.1
  166.6 42.5 all-gather.1
where the time goes:
time: 248 us
  blocking collectives  182 us (73%)
  local copies, waits for them, and re-layouts  19.8 us (8%)
  matrix products  15.2 us (6%)
  between operations  14.2 us (6%)
  loops' own time  6.26 us (3%)
  other arithmetic  5.84 us (2%)
  waiting for transfers between devices  2.89 us (1%)
    psum x1, blocking collectives, shards(): lax.psum(inner_rows(templates, templates), 'row').astype(jnp.bfloat16)  78.2 us
    psum x1, blocking collectives, own_gram(): return lax.psum(inner_rows(factor, factor), 'row')  70.9 us
    all_to_all x1, blocking collectives, shards(): lax.all_to_all(spectrogram, 'row', split_axis=1, concat_axis=0, tiled=True)  33.3 us
    concatenate x64, local copies, waits for them, and re-layouts, one_block(): jnp.concatenate([window_rows[offset:offset + block_len] for offset in ran...  11.2 us
    another operation x1, loops' own time, shards(): lax.map(one_block, jnp.arange(frame_count // block_len, dtype=jnp.int32))  6.26 us
  transfers between devices with their start and end apart: 3, of which 2 were waited for; matrix products, arithmetic and copies ran while one was open for 1% of the time, Pallas kernels for 0%

commit v1 on v0

--- a/solution.py
+++ b/solution.py
@@ -1,8 +1,12 @@
+import functools
 import math
 
 import jax
 import jax.numpy as jnp
+import numpy as np
 from jax import lax
+from jax.experimental import pallas as pl
+from jax.experimental.pallas import tpu as pltpu
 from jax.sharding import PartitionSpec as P
 
 NFFT = 8192
@@ -116,7 +120,364 @@
     return (h_new, w_new)
 
 
+LINE = 4
+STEP_FRAMES = 8
+
+
+def host_tables():
+    inner_len = NFFT // radix
+    half_len = inner_len // 2
+    two_pi = np.float32(2.0 * math.pi)
+    outer = np.arange(radix)
+    inner = np.arange(inner_len)
+    upper = np.arange(half_len)
+    one = (outer[:, None] * outer[None, :] % radix).astype(np.float32) * (two_pi / np.float32(radix))
+    table = np.concatenate([np.cos(one), -np.sin(one)], axis=1)
+    first = np.zeros((2, 2, inner_len, 2, 2 * radix), np.float32)
+    for parity in range(2):
+        for which in range(2):
+            first[parity, which, :, which, :] = table[parity::2]
+    first = first.reshape(4 * inner_len, 4 * radix)
+    twid = (inner[:, None] * outer[None, :] % NFFT).astype(np.float32) * (two_pi / np.float32(NFFT))
+    two = (inner[:, None] * upper[None, :] % inner_len).astype(np.float32) * (
+        two_pi / np.float32(inner_len)
+    )
+    cos_two, sin_two = np.cos(two), np.sin(two)
+    second = np.concatenate(
+        [
+            np.concatenate([cos_two, -sin_two], axis=1),
+            np.concatenate([sin_two, cos_two], axis=1),
+        ],
+        axis=0,
+    ).T
+    samples = np.arange(NFFT).astype(np.float32)
+    hann = np.float32(0.5) - np.float32(0.5) * np.cos(samples * (two_pi / np.float32(NFFT)))
+    hann = hann.reshape(NFFT // radix, radix)
+    return (
+        jnp.asarray(np.concatenate([hann, hann], axis=0), jnp.float32),
+        jnp.asarray(first).astype(jnp.bfloat16),
+        jnp.asarray(np.cos(twid), jnp.float32),
+        jnp.asarray(np.sin(twid), jnp.float32),
+        jnp.asarray(second).astype(jnp.bfloat16),
+    )
+
+
+def dot(left, right, left_dim=1, right_dim=0):
+    return lax.dot_general(
+        left, right, (((left_dim,), (right_dim,)), ((), ())), preferred_element_type=jnp.float32
+    )
+
+
+def fused(
+    aud, tmpl, act, hann, first, tcos, tsin, second, h_out, w_out,
+    ext, halo, mag, spec, cols, wall, hall, num_h, den_h, num_w, den_w,
+    halo_sems, w_send, w_recv, h_send, h_recv, x_send, x_recv,
+):
+    count = lax.axis_size("row")
+    me = lax.axis_index("row")
+    z, y, c = me // 4, (me // 2) % 2, me % 2
+    frames = act.shape[0]
+    bins = tmpl.shape[0]
+    planes = bins // radix
+    half = NFFT // radix // 2
+    samples = aud.shape[0]
+
+    def place(zz, yy, cc):
+        return (zz * 2 + yy) * 2 + cc
+
+    core_peer = place(z, y, 1 - c)
+    y_peer = place(z, 1 - y, c)
+
+    def send(src, dst, send_sem, recv_sem, device):
+        return pltpu.make_async_remote_copy(
+            src_ref=src,
+            dst_ref=dst,
+            send_sem=send_sem,
+            recv_sem=recv_sem,
+            device_id={"row": device},
+            device_id_type=pl.DeviceIdType.MESH,
+        )
+
+    barrier = pltpu.get_barrier_semaphore()
+    for d in range(1, count):
+        pl.semaphore_signal(
+            barrier,
+            inc=1,
+            device_id={"row": lax.rem(me + d, count)},
+            device_id_type=pl.DeviceIdType.MESH,
+        )
+    pl.semaphore_wait(barrier, count - 1)
+
+    halo_copy = send(
+        aud.at[pl.ds(0, halo.shape[0])], halo, halo_sems.at[0], halo_sems.at[1],
+        lax.rem(me + count - 1, count),
+    )
+    halo_copy.start()
+
+    def gather(buf, rows, send_sems, recv_sems):
+        def view(slot):
+            return buf.at[pl.ds(pl.multiple_of(slot * rows, rows), rows)]
+
+        def make(slot, way, device):
+            return send(
+                view(slot), view(slot), send_sems.at[way, slot], recv_sems.at[slot], device
+            )
+
+        def arrived(slot):
+            make(slot, 0, core_peer).wait_recv()
+
+        def each_send(slot_z, sign, act_on):
+            slot = place(slot_z, y, c)
+            for way, step in ((2, 1), (3, -1)):
+                if sign in (0, step):
+
+                    @pl.when((z + step >= 0) & (z + step < LINE))
+                    def _():
+                        act_on(make(slot, way, place(z + step, y, c)))
+
+            act_on(make(slot, 1, y_peer))
+            act_on(make(slot, 0, core_peer))
+
+        def over_line(d, body):
+            for sign in (1, -1):
+                from_z = z - sign * d
+
+                @pl.when((from_z >= 0) & (from_z < LINE))
+                def _():
+                    body(from_z, sign)
+
+        def start_own():
+            each_send(z, 0, lambda cp: cp.start())
+
+        def relay_line(d):
+            def body(from_z, sign):
+                arrived(place(from_z, y, c))
+                each_send(from_z, sign, lambda cp: cp.start())
+
+            over_line(d, body)
+
+        def relay_side(d):
+            def body(from_z, sign):
+                slot = place(from_z, 1 - y, c)
+                arrived(slot)
+                make(slot, 0, core_peer).start()
+
+            if d == 0:
+                body(z, 0)
+            else:
+                over_line(d, body)
+
+        def finish():
+            for zz in range(LINE):
+                for yy in range(2):
+                    arrived(place(zz, yy, 1 - c))
+
+        def drain():
+            each_send(z, 0, lambda cp: cp.wait_send())
+            make(place(z, 1 - y, c), 0, core_peer).wait_send()
+            for d in range(1, LINE):
+
+                def body(from_z, sign):
+                    each_send(from_z, sign, lambda cp: cp.wait_send())
+                    make(place(from_z, 1 - y, c), 0, core_peer).wait_send()
+
+                over_line(d, body)
+
+        return start_own, relay_line, relay_side, finish, drain
+
+    w_start, w_line, w_side, w_finish, w_drain = gather(wall, bins, w_send, w_recv)
+    h_start, h_line, h_side, h_finish, h_drain = gather(hall, frames, h_send, h_recv)
+
+    wall[pl.ds(pl.multiple_of(me * bins, bins), bins)] = tmpl[...]
+    w_start()
+    ext[pl.ds(0, samples)] = aud[...]
+
+    per_frame = HOP // radix
+    pairs = STEP_FRAMES // 2
+
+    def transform(i, carry):
+        base = pl.multiple_of(i * STEP_FRAMES * per_frame, STEP_FRAMES * per_frame)
+        lefts = []
+        for f in range(pairs):
+            block = ext[pl.ds(base + per_frame * f, radix)].astype(jnp.float32) * hann[...]
+            turned = block.astype(jnp.bfloat16).T
+            lefts.append(jnp.concatenate([turned[: radix // 2], turned[radix // 2 :]], axis=1))
+        out_one = dot(jnp.concatenate(lefts, axis=0), first[...])
+        rights = []
+        for f in range(pairs):
+            for g in range(2):
+                piece = out_one[64 * f : 64 * f + 64, 256 * g : 256 * g + 256]
+                real_y = piece[:, :radix]
+                imag_y = piece[:, radix:]
+                real_z = (real_y * tcos[...] + imag_y * tsin[...]).astype(jnp.bfloat16)
+                imag_z = (imag_y * tcos[...] - real_y * tsin[...]).astype(jnp.bfloat16)
+                rights.append(jnp.concatenate([real_z, imag_z], axis=0))
+        out_two = dot(second[...], jnp.concatenate(rights, axis=1))
+        real_x = out_two[:half]
+        imag_x = out_two[half:]
+        level = jnp.sqrt(real_x * real_x + imag_x * imag_x) * (16.0 / math.sqrt(NFFT))
+        for f in range(pairs):
+            for g in range(2):
+                j = 2 * f + g
+                frame = i * STEP_FRAMES + f + pairs * g
+                mag[pl.ds(pl.multiple_of(frame * half, half), half)] = level[
+                    :, radix * j : radix * j + radix
+                ]
+        return carry
+
+    steps = frames // STEP_FRAMES
+    cut_one, cut_two = steps // 2, steps - 1
+    lax.fori_loop(0, cut_one, transform, 0)
+    w_line(1)
+    lax.fori_loop(cut_one, cut_two, transform, 0)
+    halo_copy.wait()
+    tail = halo[...]
+    ext[pl.ds(samples, halo.shape[0])] = jnp.where(me == count - 1, jnp.zeros_like(tail), tail)
+    lax.fori_loop(cut_two, steps, transform, 0)
+    w_side(0)
+    w_line(2)
+
+    def regroup(m, carry):
+        spec[m] = mag[pl.ds(m, frames, stride=half), :].astype(jnp.bfloat16)
+        return carry
+
+    lax.fori_loop(0, half, regroup, 0)
+
+    def exchange(dz, dy, dc):
+        target = place(lax.rem(z + dz, LINE), lax.rem(y + dy, 2), lax.rem(c + dc, 2))
+        order = (dz * 2 + dy) * 2 + dc
+        return send(
+            spec.at[pl.ds(target * planes, planes)],
+            cols.at[:, pl.ds(pl.multiple_of(me * frames, frames), frames)],
+            x_send.at[order],
+            x_recv.at[me],
+            target,
+        )
+
+    def each_exchange(act_on):
+        for dz in (2, 1, 3, 0):
+            for dy in (1, 0):
+                for dc in (0, 1):
+                    if dz or dy or dc:
+                        act_on(exchange(dz, dy, dc))
+
+    each_exchange(lambda cp: cp.start())
+    cols[:, pl.ds(pl.multiple_of(me * frames, frames), frames)] = spec[
+        pl.ds(me * planes, planes)
+    ]
+    w_side(1)
+    w_line(3)
+    w_side(2)
+    w_side(3)
+    w_finish()
+
+    num_h[...] = jnp.zeros_like(num_h)
+    den_h[...] = jnp.zeros_like(den_h)
+
+    def bins_step(s, carry):
+        block = wall[pl.ds(pl.multiple_of(s * bins, bins), bins)]
+        left = jnp.concatenate([spec[s * planes + p] for p in range(planes)], axis=1)
+        num_h[...] += dot(left, block)
+        mid = dot(act[...], block, 1, 1).astype(jnp.bfloat16)
+        den_h[...] += dot(mid, block)
+        return carry
+
+    lax.fori_loop(0, count, bins_step, 0)
+    h_new = (act[...].astype(jnp.float32) * num_h[...] / den_h[...]).astype(jnp.bfloat16)
+    h_out[...] = h_new
+    hall[pl.ds(pl.multiple_of(me * frames, frames), frames)] = h_new
+    h_start()
+    h_line(1)
+    h_side(0)
+    h_line(2)
+    h_side(1)
+    h_line(3)
+    h_side(2)
+    h_side(3)
+    h_finish()
+
+    def exchanged(src):
+        send(
+            spec.at[pl.ds(0, planes)],
+            cols.at[:, pl.ds(pl.multiple_of(src * frames, frames), frames)],
+            x_send.at[0],
+            x_recv.at[src],
+            core_peer,
+        ).wait_recv()
+
+    for d in range(1, count):
+        exchanged(lax.rem(me + d, count))
+
+    num_w[...] = jnp.zeros_like(num_w)
+    den_w[...] = jnp.zeros_like(den_w)
+    chunk = 2 * frames
+
+    def frames_step(s, carry):
+        rows = pl.ds(pl.multiple_of(s * chunk, chunk), chunk)
+        block = hall[rows]
+        mid = dot(tmpl[...], block, 1, 1).astype(jnp.bfloat16)
+        den_w[...] += dot(mid, block)
+        for p in range(planes):
+            num_w[pl.ds(p * radix, radix)] += dot(cols[p, rows], block, 0, 0)
+        return carry
+
+    lax.fori_loop(0, count * frames // chunk, frames_step, 0)
+    w_out[...] = (tmpl[...].astype(jnp.float32) * num_w[...] / den_w[...]).astype(jnp.bfloat16)
+    w_drain()
+    h_drain()
+    each_exchange(lambda cp: cp.wait_send())
+
+
+def fused_shards(audio, templates, activations):
+    count = lax.axis_size("row")
+    frames, rank = activations.shape
+    bins = templates.shape[0]
+    tables = host_tables()
+    aud = audio.reshape(audio.shape[0] // radix, radix)
+    halo_rows = 3 * HOP // radix
+    low, wide = jnp.bfloat16, jnp.float32
+    vmem = pl.BlockSpec(memory_space=pltpu.VMEM)
+    dma = pltpu.SemaphoreType.DMA
+    return pl.pallas_call(
+        fused,
+        out_shape=(
+            jax.ShapeDtypeStruct(activations.shape, low),
+            jax.ShapeDtypeStruct(templates.shape, low),
+        ),
+        in_specs=[vmem] * 8,
+        out_specs=(vmem, vmem),
+        scratch_shapes=[
+            pltpu.VMEM((aud.shape[0] + halo_rows, radix), low),
+            pltpu.VMEM((halo_rows, radix), low),
+            pltpu.VMEM((frames * BINS // radix, radix), wide),
+            pltpu.VMEM((BINS // radix, frames, radix), low),
+            pltpu.VMEM((bins // radix, count * frames, radix), low),
+            pltpu.VMEM((count * bins, rank), low),
+            pltpu.VMEM((count * frames, rank), low),
+            pltpu.VMEM((frames, rank), wide),
+            pltpu.VMEM((frames, rank), wide),
+            pltpu.VMEM((bins, rank), wide),
+            pltpu.VMEM((bins, rank), wide),
+            dma((2,)),
+            dma((4, count)),
+            dma((count,)),
+            dma((4, count)),
+            dma((count,)),
+            dma((count,)),
+            dma((count,)),
+        ],
+        compiler_params=pltpu.CompilerParams(
+            collective_id=0, has_side_effects=True, vmem_limit_bytes=48 * 1024 * 1024
+        ),
+        cost_estimate=pl.CostEstimate(
+            flops=4_000_000_000, bytes_accessed=8_000_000, transcendentals=0
+        ),
+        name="spectral_nmf",
+    )(aud, templates, activations, *tables)
+
+
 def solution(mesh):
     in_specs = (P(("parts", "row")), P(("parts", "row"), None), P(("parts", "row"), None))
     out_specs = (P(("parts", "row"), None), P(("parts", "row"), None))
-    return jax.shard_map(shards, mesh=mesh, in_specs=in_specs, out_specs=out_specs, check_vma=False)
+    body = fused_shards if mesh.shape["row"] == LINE * 4 else shards
+    return jax.shard_map(body, mesh=mesh, in_specs=in_specs, out_specs=out_specs, check_vma=False)

time: 248 us -> 87 us (0.35)
  blocking collectives: 182 us -> 0 us
  Pallas kernels: 0 us -> 76.8 us
  matrix products: 15.2 us -> 0 us
  between operations: 14.2 us -> 0.65 us
  local copies, waits for them, and re-layouts: 19.8 us -> 8.27 us
  loops' own time: 6.26 us -> 0 us
  other arithmetic: 5.84 us -> 0 us
  waiting for transfers between devices: 2.89 us -> 0 us
    psum x2 -> x0, blocking collectives: 149 us -> none  [the longest x1 78.2 us: shards(): lax.psum(inner_rows(templates, templates), 'row').astype(jnp.bfloat16)]
    pallas_call x0 -> x1, Pallas kernels: none -> 76.8 us  [fused_shards(): pl.pallas_call(fused, out_shape=(jax.ShapeDtypeStruct(activations.shape,...]
    all_to_all x1 -> x0, blocking collectives: 33.3 us -> none  [shards(): lax.all_to_all(spectrogram, 'row', split_axis=1, concat_axis=0, tiled=True)]
    dot_general x22 -> x0, matrix products: 15.2 us -> none  [the longest x3 4.64 us: inner_rows(): lax.dot_general(left, right, (((0,), (0,)), ((), ())), preferred_element_...]
    concatenate x64 -> x0, local copies, waits for them, and re-layouts: 11.2 us -> none  [one_block(): jnp.concatenate([window_rows[offset:offset + block_len] for offset in ran...]
    unnamed x5 -> x18, local copies, waits for them, and re-layouts: 0.26 us -> 8.27 us
    another operation x1 -> x0, loops' own time: 6.26 us -> none  [shards(): lax.map(one_block, jnp.arange(frame_count // block_len, dtype=jnp.int32))]
    dynamic_slice x8 -> x0, local copies, waits for them, and re-layouts: 4.69 us -> none  [shards(): lax.map(one_block, jnp.arange(frame_count // block_len, dtype=jnp.int32))]
  transfers between devices with their start and end apart: 3 -> 0, of which waited for: 2 -> 0; matrix products, arithmetic and copies ran while one was open for 1% -> 0% of each run, Pallas kernels for 0% -> 0%
where the time goes in v1:
time: 87 us; the launch traced here: 85.7 us
  Pallas kernels  76.8 us (88%)
  local copies, waits for them, and re-layouts  8.27 us (10%)
    pallas_call x1, Pallas kernels, fused_shards(): pl.pallas_call(fused, out_shape=(jax.ShapeDtypeStruct(activations.shape,...  76.8 us
    unnamed x18, local copies, waits for them, and re-layouts  8.27 us

profile of v1, /device:TPU:0, one launch (start us, length us, event | category | flops | bytes accessed | tf_op | source)
XLA Modules:
  0.0 85.7 jit_solution(7928190544101798455)
XLA Ops:
  0.6 0.0 copy-start
  0.6 1.0 %copy-done = bf16[262144]{0:T(1024)(128)(2,1)S(1)} copy-done((bf16[262144]{0:T(1024)(128)(2,1)S(1)}, bf16[262144]{0:T(1024)(128)(2,1)}, u32[]{:S(2)}) %copy-start) | copy-done | bytes 524312
  1.7 0.0 copy-start.1
  1.7 0.9 %copy-done.1 = bf16[256,512]{1,0:T(8,128)(2,1)S(1)} copy-done((bf16[256,512]{1,0:T(8,128)(2,1)S(1)}, bf16[256,512]{1,0:T(8,128)(2,1)}, u32[]{:S(2)}) %copy-start.1) | copy-done | bytes 262168
  2.6 0.0 copy-start.2
  2.6 0.9 %copy-done.2 = bf16[128,512]{1,0:T(8,128)(2,1)S(1)} copy-done((bf16[128,512]{1,0:T(8,128)(2,1)S(1)}, bf16[128,512]{1,0:T(8,128)(2,1)}, u32[]{:S(2)}) %copy-start.2) | copy-done | bytes 131096
  3.5 0.0 copy-start.3
  3.5 0.9 %copy-done.3 = bf16[256,512]{1,0:T(8,128)(2,1)S(1)} copy-done((bf16[256,512]{1,0:T(8,128)(2,1)S(1)}, bf16[256,512]{1,0:T(8,128)(2,1)}, u32[]{:S(2)}) %copy-start.3) | copy-done | bytes 262168
  4.5 0.0 copy-start.4
  4.5 0.8 copy-done.4
  5.3 0.0 copy-start.5
  5.3 0.8 copy-done.5
  6.1 0.0 copy-start.6
  6.1 0.8 copy-done.6
  6.8 0.0 copy-start.7
  6.8 0.7 copy-done.7
  7.6 76.8 %spectral_nmf.1 = (bf16[128,512]{1,0:T(8,128)(2,1)S(1)}, bf16[256,512]{1,0:T(8,128)(2,1)S(1)}) custom-call(bf16[2048,128]{1,0:T(8,128)(2,1)S(1)} %bitcast.1, bf16[256,512]{1,0:T(8,128)(2,1)S(1)} %copy-done.1, bf16[128,512]{1,0:T(8,128)(2,1)S(1)} %copy-done.2, f32[128,128]{1,0:T(8,128)S(1)} %copy-done.4, bf16[256,512]{1,0:T(8,128)(2,1)S(1)} %copy-done.3, ...), custom_call_target="tpu_custom_call" | custom-call | flops 4000000000 | bytes 8000000 | tf_op jit(solution)/shard_map/spectral_nmf/pallas_call | solution.py:441
  84.3 0.7 copy.12
  85.0 0.7 copy.13
Async XLA Ops:
  0.6 1.0 %copy-start = (bf16[262144]{0:T(1024)(128)(2,1)S(1)}, bf16[262144]{0:T(1024)(128)(2,1)}, u32[]{:S(2)}) copy-start(bf16[262144]{0:T(1024)(128)(2,1)} %param.8) | copy-start | bytes 1572868
  1.7 0.9 %copy-start.1 = (bf16[256,512]{1,0:T(8,128)(2,1)S(1)}, bf16[256,512]{1,0:T(8,128)(2,1)}, u32[]{:S(2)}) copy-start(bf16[256,512]{1,0:T(8,128)(2,1)} %tmpl.1) | copy-start | bytes 786436
  2.6 0.9 %copy-start.2 = (bf16[128,512]{1,0:T(8,128)(2,1)S(1)}, bf16[128,512]{1,0:T(8,128)(2,1)}, u32[]{:S(2)}) copy-start(bf16[128,512]{1,0:T(8,128)(2,1)} %act.1) | copy-start | bytes 393220
  3.5 0.9 %copy-start.3 = (bf16[256,512]{1,0:T(8,128)(2,1)S(1)}, bf16[256,512]{1,0:T(8,128)(2,1)}, u32[]{:S(2)}) copy-start(bf16[256,512]{1,0:T(8,128)(2,1)} %constant.15.first) | copy-start | bytes 786436
  4.5 0.8 copy-start.4
  5.3 0.8 copy-start.5
  6.1 0.8 copy-start.6
  6.8 0.7 copy-start.7

commit v2 on v1

--- a/solution.py
+++ b/solution.py
@@ -122,6 +122,9 @@
 
 LINE = 4
 STEP_FRAMES = 8
+W_PIECES = 2
+H_PIECES = 2
+EXCHANGE = ((0,), (2,), (1, 3), ())
 
 
 def host_tables():
@@ -169,18 +172,19 @@
 
 
 def fused(
-    aud, tmpl, act, hann, first, tcos, tsin, second, h_out, w_out,
+    aud_in, tmpl_in, act_in, hann_in, first_in, tcos_in, tsin_in, second_in, h_out, w_out,
+    act, hann, first, tcos, tsin, second,
     ext, halo, mag, spec, cols, wall, hall, num_h, den_h, num_w, den_w,
-    halo_sems, w_send, w_recv, h_send, h_recv, x_send, x_recv,
+    load_sems, halo_sems, w_send, w_recv, h_send, h_recv, x_send, x_recv,
 ):
     count = lax.axis_size("row")
     me = lax.axis_index("row")
     z, y, c = me // 4, (me // 2) % 2, me % 2
-    frames = act.shape[0]
-    bins = tmpl.shape[0]
+    frames = act_in.shape[0]
+    bins = tmpl_in.shape[0]
     planes = bins // radix
     half = NFFT // radix // 2
-    samples = aud.shape[0]
+    samples = aud_in.shape[0]
 
     def place(zz, yy, cc):
         return (zz * 2 + yy) * 2 + cc
@@ -198,6 +202,26 @@
             device_id_type=pl.DeviceIdType.MESH,
         )
 
+    own_bins = pl.ds(pl.multiple_of(me * bins, bins), bins)
+    own_frames = pl.ds(pl.multiple_of(me * frames, frames), frames)
+    loads = [
+        pltpu.make_async_copy(src, dst, load_sems.at[i])
+        for i, (src, dst) in enumerate(
+            (
+                (tmpl_in, wall.at[own_bins]),
+                (aud_in, ext.at[pl.ds(0, samples)]),
+                (hann_in, hann),
+                (first_in, first),
+                (tcos_in, tcos),
+                (tsin_in, tsin),
+                (second_in, second),
+                (act_in, act),
+            )
+        )
+    ]
+    for load in loads:
+        load.start()
+
     barrier = pltpu.get_barrier_semaphore()
     for d in range(1, count):
         pl.semaphore_signal(
@@ -209,36 +233,38 @@
     pl.semaphore_wait(barrier, count - 1)
 
     halo_copy = send(
-        aud.at[pl.ds(0, halo.shape[0])], halo, halo_sems.at[0], halo_sems.at[1],
+        aud_in.at[pl.ds(0, halo.shape[0])], halo, halo_sems.at[0], halo_sems.at[1],
         lax.rem(me + count - 1, count),
     )
     halo_copy.start()
 
-    def gather(buf, rows, send_sems, recv_sems):
-        def view(slot):
-            return buf.at[pl.ds(pl.multiple_of(slot * rows, rows), rows)]
-
-        def make(slot, way, device):
-            return send(
-                view(slot), view(slot), send_sems.at[way, slot], recv_sems.at[slot], device
-            )
-
-        def arrived(slot):
-            make(slot, 0, core_peer).wait_recv()
-
-        def each_send(slot_z, sign, act_on):
+    def gather(buf, rows, pieces, send_sems, recv_sems):
+        size = rows // pieces
+
+        def make(slot, q, way, device):
+            unit = slot * pieces + q
+            view = buf.at[pl.ds(pl.multiple_of(unit * size, size), size)]
+            return send(view, view, send_sems.at[way, unit], recv_sems.at[unit], device)
+
+        def arrived(slot, q):
+            make(slot, q, 0, core_peer).wait_recv()
+
+        def each_send(slot_z, q, sign, act_on):
             slot = place(slot_z, y, c)
             for way, step in ((2, 1), (3, -1)):
                 if sign in (0, step):
 
                     @pl.when((z + step >= 0) & (z + step < LINE))
                     def _():
-                        act_on(make(slot, way, place(z + step, y, c)))
-
-            act_on(make(slot, 1, y_peer))
-            act_on(make(slot, 0, core_peer))
+                        act_on(make(slot, q, way, place(z + step, y, c)))
+
+            act_on(make(slot, q, 1, y_peer))
+            act_on(make(slot, q, 0, core_peer))
 
         def over_line(d, body):
+            if d == 0:
+                body(z, 0)
+                return
             for sign in (1, -1):
                 from_z = z - sign * d
 
@@ -247,50 +273,56 @@
                     body(from_z, sign)
 
         def start_own():
-            each_send(z, 0, lambda cp: cp.start())
+            for q in range(pieces):
+                each_send(z, q, 0, lambda cp: cp.start())
 
         def relay_line(d):
+            for q in range(pieces):
+
+                def body(from_z, sign):
+                    arrived(place(from_z, y, c), q)
+                    each_send(from_z, q, sign, lambda cp: cp.start())
+
+                over_line(d, body)
+
+        def relay_side(d):
+            for q in range(pieces):
+
+                def body(from_z, sign):
+                    slot = place(from_z, 1 - y, c)
+                    arrived(slot, q)
+                    make(slot, q, 0, core_peer).start()
+
+                over_line(d, body)
+
+        def plane(d, process):
             def body(from_z, sign):
-                arrived(place(from_z, y, c))
-                each_send(from_z, sign, lambda cp: cp.start())
+                for q in range(pieces):
+                    for yy in range(2):
+                        arrived(place(from_z, yy, 1 - c), q)
+                process(from_z)
 
             over_line(d, body)
 
-        def relay_side(d):
-            def body(from_z, sign):
-                slot = place(from_z, 1 - y, c)
-                arrived(slot)
-                make(slot, 0, core_peer).start()
-
-            if d == 0:
-                body(z, 0)
-            else:
-                over_line(d, body)
-
-        def finish():
-            for zz in range(LINE):
-                for yy in range(2):
-                    arrived(place(zz, yy, 1 - c))
-
         def drain():
-            each_send(z, 0, lambda cp: cp.wait_send())
-            make(place(z, 1 - y, c), 0, core_peer).wait_send()
-            for d in range(1, LINE):
-
-                def body(from_z, sign):
-                    each_send(from_z, sign, lambda cp: cp.wait_send())
-                    make(place(from_z, 1 - y, c), 0, core_peer).wait_send()
-
-                over_line(d, body)
-
-        return start_own, relay_line, relay_side, finish, drain
-
-    w_start, w_line, w_side, w_finish, w_drain = gather(wall, bins, w_send, w_recv)
-    h_start, h_line, h_side, h_finish, h_drain = gather(hall, frames, h_send, h_recv)
-
-    wall[pl.ds(pl.multiple_of(me * bins, bins), bins)] = tmpl[...]
+            for q in range(pieces):
+                for d in range(LINE):
+
+                    def body(from_z, sign):
+                        each_send(from_z, q, sign, lambda cp: cp.wait_send())
+                        make(place(from_z, 1 - y, c), q, 0, core_peer).wait_send()
+
+                    over_line(d, body)
+
+        return start_own, relay_line, relay_side, plane, drain
+
+    w_start, w_line, w_side, w_plane, w_drain = gather(wall, bins, W_PIECES, w_send, w_recv)
+    h_start, h_line, h_side, h_plane, h_drain = gather(hall, frames, H_PIECES, h_send, h_recv)
+
+    loads[0].wait()
     w_start()
-    ext[pl.ds(0, samples)] = aud[...]
+    for load in loads[1:]:
+        load.wait()
 
     per_frame = HOP // radix
     pairs = STEP_FRAMES // 2
@@ -326,16 +358,12 @@
         return carry
 
     steps = frames // STEP_FRAMES
-    cut_one, cut_two = steps // 2, steps - 1
-    lax.fori_loop(0, cut_one, transform, 0)
-    w_line(1)
-    lax.fori_loop(cut_one, cut_two, transform, 0)
+    lax.fori_loop(0, steps - 1, transform, 0)
     halo_copy.wait()
     tail = halo[...]
     ext[pl.ds(samples, halo.shape[0])] = jnp.where(me == count - 1, jnp.zeros_like(tail), tail)
-    lax.fori_loop(cut_two, steps, transform, 0)
-    w_side(0)
-    w_line(2)
+    lax.fori_loop(steps - 1, steps, transform, 0)
+    w_line(1)
 
     def regroup(m, carry):
         spec[m] = mag[pl.ds(m, frames, stride=half), :].astype(jnp.bfloat16)
@@ -354,47 +382,48 @@
             target,
         )
 
-    def each_exchange(act_on):
-        for dz in (2, 1, 3, 0):
-            for dy in (1, 0):
-                for dc in (0, 1):
-                    if dz or dy or dc:
-                        act_on(exchange(dz, dy, dc))
-
-    each_exchange(lambda cp: cp.start())
-    cols[:, pl.ds(pl.multiple_of(me * frames, frames), frames)] = spec[
-        pl.ds(me * planes, planes)
-    ]
-    w_side(1)
-    w_line(3)
-    w_side(2)
-    w_side(3)
-    w_finish()
+    def each_exchange(dz, act_on):
+        for dy in (1, 0):
+            for dc in (0, 1):
+                if dz or dy or dc:
+                    act_on(exchange(dz, dy, dc))
 
     num_h[...] = jnp.zeros_like(num_h)
     den_h[...] = jnp.zeros_like(den_h)
 
-    def bins_step(s, carry):
-        block = wall[pl.ds(pl.multiple_of(s * bins, bins), bins)]
-        left = jnp.concatenate([spec[s * planes + p] for p in range(planes)], axis=1)
+    def bins_plane(zz):
+        span = 4 * bins
+        block = wall[pl.ds(pl.multiple_of(zz * span, span), span)]
+        first_plane = zz * (4 * planes)
+        left = jnp.concatenate([spec[first_plane + p] for p in range(4 * planes)], axis=1)
+        mid = dot(act[...], block, 1, 1).astype(jnp.bfloat16)
         num_h[...] += dot(left, block)
-        mid = dot(act[...], block, 1, 1).astype(jnp.bfloat16)
         den_h[...] += dot(mid, block)
-        return carry
-
-    lax.fori_loop(0, count, bins_step, 0)
+
+    def start_exchange(point):
+        for dz in EXCHANGE[point]:
+            each_exchange(dz, lambda cp: cp.start())
+
+    start_exchange(0)
+    cols[:, own_frames] = spec[pl.ds(me * planes, planes)]
+    w_side(0)
+    w_plane(0, bins_plane)
+    w_line(2)
+    start_exchange(1)
+    w_side(1)
+    w_plane(1, bins_plane)
+    w_line(3)
+    start_exchange(2)
+    w_side(2)
+    w_plane(2, bins_plane)
+    w_side(3)
+    w_plane(3, bins_plane)
+
     h_new = (act[...].astype(jnp.float32) * num_h[...] / den_h[...]).astype(jnp.bfloat16)
     h_out[...] = h_new
-    hall[pl.ds(pl.multiple_of(me * frames, frames), frames)] = h_new
+    hall[own_frames] = h_new
     h_start()
-    h_line(1)
-    h_side(0)
-    h_line(2)
-    h_side(1)
-    h_line(3)
-    h_side(2)
-    h_side(3)
-    h_finish()
+    start_exchange(3)
 
     def exchanged(src):
         send(
@@ -405,27 +434,48 @@
             core_peer,
         ).wait_recv()
 
-    for d in range(1, count):
-        exchanged(lax.rem(me + d, count))
-
     num_w[...] = jnp.zeros_like(num_w)
     den_w[...] = jnp.zeros_like(den_w)
-    chunk = 2 * frames
-
-    def frames_step(s, carry):
-        rows = pl.ds(pl.multiple_of(s * chunk, chunk), chunk)
-        block = hall[rows]
-        mid = dot(tmpl[...], block, 1, 1).astype(jnp.bfloat16)
+
+    def plane_rows(zz):
+        span = 4 * frames
+        return pl.ds(pl.multiple_of(zz * span, span), span)
+
+    def gram_plane(zz):
+        block = hall[plane_rows(zz)]
+        mid = dot(wall[own_bins], block, 1, 1).astype(jnp.bfloat16)
         den_w[...] += dot(mid, block)
+
+    def frames_plane(zz):
+        rows = plane_rows(zz)
         for p in range(planes):
-            num_w[pl.ds(p * radix, radix)] += dot(cols[p, rows], block, 0, 0)
-        return carry
-
-    lax.fori_loop(0, count * frames // chunk, frames_step, 0)
-    w_out[...] = (tmpl[...].astype(jnp.float32) * num_w[...] / den_w[...]).astype(jnp.bfloat16)
+            num_w[pl.ds(p * radix, radix)] += dot(cols[p, rows], hall[rows], 0, 0)
+
+    h_line(1)
+    h_side(0)
+    h_line(2)
+    h_plane(0, gram_plane)
+    h_side(1)
+    h_line(3)
+    h_plane(1, gram_plane)
+    h_side(2)
+    h_side(3)
+    for dz in (0, 1, 3, 2):
+        for dy in range(2):
+            for dc in range(2):
+                if dz or dy or dc:
+                    exchanged(place(lax.rem(z + dz, LINE), lax.rem(y + dy, 2), lax.rem(c + dc, 2)))
+        if dz == 0:
+            frames_plane(z)
+    h_plane(2, gram_plane)
+    h_plane(3, gram_plane)
+    for dz in (1, 3, 2):
+        frames_plane(lax.rem(z + dz, LINE))
+    w_out[...] = (wall[own_bins].astype(jnp.float32) * num_w[...] / den_w[...]).astype(jnp.bfloat16)
     w_drain()
     h_drain()
-    each_exchange(lambda cp: cp.wait_send())
+    for dz in range(LINE):
+        each_exchange(dz, lambda cp: cp.wait_send())
 
 
 def fused_shards(audio, templates, activations):
@@ -444,9 +494,11 @@
             jax.ShapeDtypeStruct(activations.shape, low),
             jax.ShapeDtypeStruct(templates.shape, low),
         ),
-        in_specs=[vmem] * 8,
+        in_specs=[pl.BlockSpec(memory_space=pl.ANY)] * 8,
         out_specs=(vmem, vmem),
         scratch_shapes=[
+            pltpu.VMEM(activations.shape, low),
+            *(pltpu.VMEM(table.shape, table.dtype) for table in tables),
             pltpu.VMEM((aud.shape[0] + halo_rows, radix), low),
             pltpu.VMEM((halo_rows, radix), low),
             pltpu.VMEM((frames * BINS // radix, radix), wide),
@@ -458,16 +510,17 @@
             pltpu.VMEM((frames, rank), wide),
             pltpu.VMEM((bins, rank), wide),
             pltpu.VMEM((bins, rank), wide),
+            dma((8,)),
             dma((2,)),
-            dma((4, count)),
-            dma((count,)),
-            dma((4, count)),
-            dma((count,)),
+            dma((4, count * W_PIECES)),
+            dma((count * W_PIECES,)),
+            dma((4, count * H_PIECES)),
+            dma((count * H_PIECES,)),
             dma((count,)),
             dma((count,)),
         ],
         compiler_params=pltpu.CompilerParams(
-            collective_id=0, has_side_effects=True, vmem_limit_bytes=48 * 1024 * 1024
+            collective_id=0, has_side_effects=True, vmem_limit_bytes=60 * 1024 * 1024
         ),
         cost_estimate=pl.CostEstimate(
             flops=4_000_000_000, bytes_accessed=8_000_000, transcendentals=0

time: 87 us -> 69.2 us (0.80); the launches traced: 85.7 us -> 69.1 us
  Pallas kernels: 76.8 us -> 66.1 us
  local copies, waits for them, and re-layouts: 8.27 us -> 2.32 us
    pallas_call x1, Pallas kernels: 76.8 us -> 66.1 us  [fused_shards(): pl.pallas_call(fused, out_shape=(jax.ShapeDtypeStruct(activations.shape,...]
    unnamed x18 -> x4, local copies, waits for them, and re-layouts: 8.27 us -> 2.32 us
where the time goes in v2:
time: 69.2 us; the launch traced here: 69.1 us
  Pallas kernels  66.1 us (96%)
  local copies, waits for them, and re-layouts  2.32 us (3%)
    pallas_call x1, Pallas kernels, fused_shards(): pl.pallas_call(fused, out_shape=(jax.ShapeDtypeStruct(activations.shape,...  66.1 us
    unnamed x4, local copies, waits for them, and re-layouts  2.32 us

profile of v2, /device:TPU:0, one launch (start us, length us, event | category | flops | bytes accessed | tf_op | source)
XLA Modules:
  0.0 69.1 jit_solution(202079816922910789)
XLA Ops:
  0.6 66.1 %spectral_nmf.1 = (bf16[128,512]{1,0:T(8,128)(2,1)}, bf16[256,512]{1,0:T(8,128)(2,1)}) custom-call(bf16[2048,128]{1,0:T(8,128)(2,1)} %bitcast.1, bf16[256,512]{1,0:T(8,128)(2,1)} %tmpl_in.1, bf16[128,512]{1,0:T(8,128)(2,1)} %act_in.1, f32[128,128]{1,0:T(8,128)} %constant.10.clone.hann_in, bf16[256,512]{1,0:T(8,128)(2,1)} %constant.15.first_in, ...), custom_call_target="tpu_custom_call" | custom-call | flops 4000000000 | bytes 8000000 | tf_op jit(solution)/shard_map/spectral_nmf/pallas_call | solution.py:491
  66.7 0.0 copy-start
  66.7 1.6 %copy.12 = bf16[128,512]{1,0:T(8,128)(2,1)} copy(bf16[128,512]{1,0:T(8,128)(2,1)} %get-tuple-element.4) | data formatting | bytes 262144
  68.3 0.0 copy-done
  68.4 0.7 %copy.13 = bf16[256,512]{1,0:T(8,128)(2,1)} copy(bf16[256,512]{1,0:T(8,128)(2,1)S(1)} %copy-done) | data formatting | bytes 524288
Async XLA Ops:
  66.7 1.6 %copy-start = (bf16[256,512]{1,0:T(8,128)(2,1)S(1)}, bf16[256,512]{1,0:T(8,128)(2,1)}, u32[]{:S(2)}) copy-start(bf16[256,512]{1,0:T(8,128)(2,1)} %get-tuple-element.5) | copy-start | bytes 786436

commit v3 on v2

--- a/solution.py
+++ b/solution.py
@@ -124,7 +124,7 @@
 STEP_FRAMES = 8
 W_PIECES = 2
 H_PIECES = 2
-EXCHANGE = ((0,), (2,), (1, 3), ())
+EXCHANGE = ((), (2,), (1, 3), (0,))
 
 
 def host_tables():
@@ -358,12 +358,13 @@
         return carry
 
     steps = frames // STEP_FRAMES
-    lax.fori_loop(0, steps - 1, transform, 0)
+    lax.fori_loop(0, steps // 2, transform, 0)
+    w_line(1)
+    lax.fori_loop(steps // 2, steps - 1, transform, 0)
     halo_copy.wait()
     tail = halo[...]
     ext[pl.ds(samples, halo.shape[0])] = jnp.where(me == count - 1, jnp.zeros_like(tail), tail)
     lax.fori_loop(steps - 1, steps, transform, 0)
-    w_line(1)
 
     def regroup(m, carry):
         spec[m] = mag[pl.ds(m, frames, stride=half), :].astype(jnp.bfloat16)
@@ -407,13 +408,13 @@
     start_exchange(0)
     cols[:, own_frames] = spec[pl.ds(me * planes, planes)]
     w_side(0)
-    w_plane(0, bins_plane)
     w_line(2)
     start_exchange(1)
+    w_plane(0, bins_plane)
     w_side(1)
-    w_plane(1, bins_plane)
     w_line(3)
     start_exchange(2)
+    w_plane(1, bins_plane)
     w_side(2)
     w_plane(2, bins_plane)
     w_side(3)

time: 69.2 us -> 65.6 us (0.948)
  Pallas kernels: 66.1 us -> 62.5 us
    pallas_call x1, Pallas kernels: 66.1 us -> 62.5 us  [fused_shards(): pl.pallas_call(fused, out_shape=(jax.ShapeDtypeStruct(activations.shape,...]
where the time goes in v3:
time: 65.6 us; the launch traced here: 65.5 us
  Pallas kernels  62.5 us (95%)
  local copies, waits for them, and re-layouts  2.32 us (4%)
    pallas_call x1, Pallas kernels, fused_shards(): pl.pallas_call(fused, out_shape=(jax.ShapeDtypeStruct(activations.shape,...  62.5 us
    unnamed x4, local copies, waits for them, and re-layouts  2.32 us

profile of v3, /device:TPU:0, one launch (start us, length us, event | category | flops | bytes accessed | tf_op | source)
XLA Modules:
  0.0 65.5 jit_solution(9501298671847855120)
XLA Ops:
  0.6 62.5 %spectral_nmf.1 = (bf16[128,512]{1,0:T(8,128)(2,1)}, bf16[256,512]{1,0:T(8,128)(2,1)}) custom-call(bf16[2048,128]{1,0:T(8,128)(2,1)} %bitcast.1, bf16[256,512]{1,0:T(8,128)(2,1)} %tmpl_in.1, bf16[128,512]{1,0:T(8,128)(2,1)} %act_in.1, f32[128,128]{1,0:T(8,128)} %constant.10.clone.hann_in, bf16[256,512]{1,0:T(8,128)(2,1)} %constant.15.first_in, ...), custom_call_target="tpu_custom_call" | custom-call | flops 4000000000 | bytes 8000000 | tf_op jit(solution)/shard_map/spectral_nmf/pallas_call | solution.py:492
  63.2 0.0 copy-start
  63.2 1.6 %copy.12 = bf16[128,512]{1,0:T(8,128)(2,1)} copy(bf16[128,512]{1,0:T(8,128)(2,1)} %get-tuple-element.4) | data formatting | bytes 262144
  64.8 0.0 copy-done
  64.8 0.7 %copy.13 = bf16[256,512]{1,0:T(8,128)(2,1)} copy(bf16[256,512]{1,0:T(8,128)(2,1)S(1)} %copy-done) | data formatting | bytes 524288
Async XLA Ops:
  63.2 1.6 %copy-start = (bf16[256,512]{1,0:T(8,128)(2,1)S(1)}, bf16[256,512]{1,0:T(8,128)(2,1)}, u32[]{:S(2)}) copy-start(bf16[256,512]{1,0:T(8,128)(2,1)} %get-tuple-element.5) | copy-start | bytes 786436

commit v4 on v3

--- a/solution.py
+++ b/solution.py
@@ -124,7 +124,7 @@
 STEP_FRAMES = 8
 W_PIECES = 2
 H_PIECES = 2
-EXCHANGE = ((), (2,), (1, 3), (0,))
+EXCHANGE = ((2,), (), (1, 3), (0,))
 
 
 def host_tables():
@@ -460,6 +460,7 @@
     h_line(3)
     h_plane(1, gram_plane)
     h_side(2)
+    h_plane(2, gram_plane)
     h_side(3)
     for dz in (0, 1, 3, 2):
         for dy in range(2):
@@ -468,7 +469,6 @@
                     exchanged(place(lax.rem(z + dz, LINE), lax.rem(y + dy, 2), lax.rem(c + dc, 2)))
         if dz == 0:
             frames_plane(z)
-    h_plane(2, gram_plane)
     h_plane(3, gram_plane)
     for dz in (1, 3, 2):
         frames_plane(lax.rem(z + dz, LINE))

time: 65.6 us -> 65.4 us (level)
  no operation moved by 1% of the time
where the time goes in v4:
time: 65.4 us; the launch traced here: 64.9 us
  Pallas kernels  61.9 us (95%)
  local copies, waits for them, and re-layouts  2.32 us (4%)
    pallas_call x1, Pallas kernels, fused_shards(): pl.pallas_call(fused, out_shape=(jax.ShapeDtypeStruct(activations.shape,...  61.9 us
    unnamed x4, local copies, waits for them, and re-layouts  2.32 us

profile of v4, /device:TPU:0, one launch (start us, length us, event | category | flops | bytes accessed | tf_op | source)
XLA Modules:
  0.0 64.9 jit_solution(11628807150860919508)
XLA Ops:
  0.6 61.9 %spectral_nmf.1 = (bf16[128,512]{1,0:T(8,128)(2,1)}, bf16[256,512]{1,0:T(8,128)(2,1)}) custom-call(bf16[2048,128]{1,0:T(8,128)(2,1)} %bitcast.1, bf16[256,512]{1,0:T(8,128)(2,1)} %tmpl_in.1, bf16[128,512]{1,0:T(8,128)(2,1)} %act_in.1, f32[128,128]{1,0:T(8,128)} %constant.10.clone.hann_in, bf16[256,512]{1,0:T(8,128)(2,1)} %constant.15.first_in, ...), custom_call_target="tpu_custom_call" | custom-call | flops 4000000000 | bytes 8000000 | tf_op jit(solution)/shard_map/spectral_nmf/pallas_call | solution.py:492
  62.5 0.0 copy-start
  62.5 1.6 %copy.12 = bf16[128,512]{1,0:T(8,128)(2,1)} copy(bf16[128,512]{1,0:T(8,128)(2,1)} %get-tuple-element.4) | data formatting | bytes 262144
  64.1 0.0 copy-done
  64.2 0.7 %copy.13 = bf16[256,512]{1,0:T(8,128)(2,1)} copy(bf16[256,512]{1,0:T(8,128)(2,1)S(1)} %copy-done) | data formatting | bytes 524288
Async XLA Ops:
  62.5 1.6 %copy-start = (bf16[256,512]{1,0:T(8,128)(2,1)S(1)}, bf16[256,512]{1,0:T(8,128)(2,1)}, u32[]{:S(2)}) copy-start(bf16[256,512]{1,0:T(8,128)(2,1)} %get-tuple-element.5) | copy-start | bytes 786436
